TPU v7x, 32 devices: a whole 2x2x4 slice. The times are simulated.
32 devices in a mesh: seg: 8 (over y, x, core), sub: 4 (over z).
Axes of the slice: x: 2, y: 2, z: 4, core: 2. Of those that a mesh axis runs over, the one named last changes fastest.
Arguments:
- fields: float32 [7, 256, 512], P(None, 'seg', 'sub'), may hold values from -1.5 to 3, as said below
- region_levels: int32 [8, 4], replicated, may hold values from 0 to 2, as said below
Outputs:
- new_fields: float32 [7, 256, 512], P(None, 'seg', 'sub')
Inputs may be any that keep to these rules, and one draw needn't show every extreme that they name: `region_levels`: root regions sharing a side or a corner differ by at most one level; some root region is at level 2. `fields`: component 0 (density) lies between 1 and 3; tile entries in a tile's unused room are not read.
All inputs are finite; a program needn't handle non-finite values.
Results may differ from a plain program's by a relative error of at most 0.0003.
Values sent between devices are 32-bit elements; how exact they have to be, the bound alone decides.
A program may use at most 64 MiB of HBM per device.

v0:
```python
import functools

import jax
import jax.numpy as jnp
from jax import lax
from jax.experimental import pallas as pl
from jax.experimental.pallas import tpu as pltpu
from jax.sharding import PartitionSpec as P

STEP_SIZE = 0.08
MESH = pl.DeviceIdType.MESH
F32, BF16, I32 = jnp.float32, jnp.bfloat16, jnp.int32
ROWS, COLS = 32, 128
AROUND = [(1, 0), (1, 1), (1, -1), (-1, 0), (-1, 1), (-1, -1), (0, -1), (0, 1)]


def iota(shape, axis):
    return lax.broadcasted_iota(I32, shape, axis)


def pick(level, values):
    return jnp.where(level == 0, values[0], jnp.where(level == 1, values[1], values[2]))


def halves(value, axis):
    high = value.astype(BF16)
    low = (value - high.astype(F32)).astype(BF16)
    return jnp.concatenate([high, low], axis=axis)


def dot(a, b, dims=((1,), (0,))):
    return lax.dot_general(a, b, (dims, ((), ())), preferred_element_type=F32)


def twice(matrix, axis):
    matrix = matrix.astype(BF16)
    return jnp.concatenate([matrix, matrix], axis=axis)


def resample(source, target, delta):
    source = jnp.where(delta < 0, source >> 1, source)
    target = jnp.where(delta > 0, target >> 1, target)
    return jnp.where(source == target, jnp.where(delta < 0, 0.5, 1.0), 0.0).astype(F32)


def roll(value, shift, axis):
    return pltpu.roll(value, shift % value.shape[axis], axis)


def minmod(a, b):
    return jnp.maximum(jnp.minimum(a, b), 0.0) + jnp.minimum(jnp.maximum(a, b), 0.0)


def sweep(primitives, normal, axis):
    left, right = [], []
    for value in primitives:
        before = value - roll(value, 1, axis)
        half = 0.5 * minmod(before, roll(before, -1, axis))
        left.append(roll(value + half, 1, axis))
        right.append(value - half)

    def pieces(values):
        density, speed_n, speed_t, speed_z, field_t, field_z = values
        square = normal * normal + field_t * field_t + field_z * field_z
        moment = density * speed_n
        cons = [density, moment, density * speed_t, density * speed_z, field_t, field_z]
        flux = [
            moment,
            moment * speed_n + (density + 0.5 * square) - normal * normal,
            moment * speed_t - normal * field_t,
            moment * speed_z - normal * field_z,
            field_t * speed_n - normal * speed_t,
            field_z * speed_n - normal * speed_z,
        ]
        return flux, cons, jnp.abs(speed_n) + jnp.sqrt(1.0 + square / density)

    flux_l, cons_l, signal_l = pieces(left)
    flux_r, cons_r, signal_r = pieces(right)
    fastest = jnp.maximum(signal_l, signal_r)
    return [
        0.5 * ((fl + fr) - fastest * (cr - cl))
        for fl, fr, cl, cr in zip(flux_l, flux_r, cons_l, cons_r)
    ]


def strip_choices(block, upper, sub8, odd_lane):
    same, coarse, fine = block, [], []
    sign = 1 if upper else -1
    edge = 7 if upper else 0
    for comp in range(7):
        value = block[comp]
        if comp == 6:
            pair = roll(value, 1, 0) if upper else value
        else:
            pair = 0.5 * (value + roll(value, sign, 0))
        if comp == 5:
            pair = jnp.where(odd_lane, roll(pair, 1, 1), pair)
        coarse.append(
            jnp.where(
                sub8 == edge,
                pair,
                jnp.where(sub8 == edge - sign, roll(pair, sign, 0), roll(pair, 2 * sign, 0)),
            )
        )
        fine.append(jnp.where(sub8 == edge, value, roll(value, -sign, 0)))
    return same, coarse, fine


def kernel(
    seg_count, sub_count, fields, levels, out,
    ghosted, current, row_out, row_in, col_out, col_in, line_out, line_in,
    lane_maps, row_maps, send_sem, recv_sem,
):
    seg, sub = lax.axis_index("seg"), lax.axis_index("sub")

    def place(offset):
        return (
            lax.rem(seg + (seg_count + offset[0]), seg_count),
            lax.rem(sub + (sub_count + offset[1]), sub_count),
        )

    places = [place(offset) for offset in AROUND]
    barrier = pltpu.get_barrier_semaphore()
    for target in places:
        pl.semaphore_signal(barrier, inc=1, device_id=target, device_id_type=MESH)

    level = levels[seg, sub]
    near = {offset: levels[p[0], p[1]] for offset, p in zip(AROUND, places)}
    rows = pick(level, (8, 16, 32))
    cols = pick(level, (32, 64, 128))
    ratio = pick(level, [jnp.float32(STEP_SIZE / h) for h in (4.0, 2.0, 1.0)])
    delta = {offset: near[offset] - level for offset in AROUND}

    i, j = iota((COLS, COLS), 0), iota((COLS, COLS), 1)
    for k, offset in enumerate(AROUND[:6]):
        if offset[1] == 0:
            matrix = resample(i, j, delta[offset])
        elif offset[1] == 1:
            matrix = jnp.where(j >= 125, resample(i - cols, j - COLS, delta[offset]), 0.0)
        else:
            first = j - pick(near[offset], (32, 64, 0))
            ok = (first >= 0) & (first < 3)
            matrix = jnp.where(ok, resample(i, first, delta[offset]), 0.0)
        lane_maps[k] = twice(matrix, 0)
    i, j = iota((256, 256), 0), iota((256, 256), 1)
    together = (i >> 5) == (j >> 5)
    face_rows = (i >> 5) == 6
    i, j = i & 31, j & 31
    for k, offset in enumerate(AROUND[6:]):
        d = delta[offset]
        faces = jnp.where(d < 0, jnp.where(i == 2 * j, 1.0, 0.0), resample(i, j, d))
        matrix = jnp.where(together, jnp.where(face_rows, faces, resample(i, j, d)), 0.0)
        row_maps[k] = twice(matrix, 0)
    k, i = iota((16, COLS), 0), iota((16, COLS), 1)
    to_right = k >= 8
    k = k & 7
    is_face = k >= 3
    k = k - jnp.where(is_face, 3, 0) - jnp.where(to_right, 3, 0)
    i = i - jnp.where(to_right, cols, 0)

    def column_pick(d):
        faces = jnp.where(d < 0, jnp.where(i == 2 * k, 1.0, 0.0), resample(i, k, d))
        return jnp.where(is_face, faces, resample(i, k, d))

    column_map = twice(
        jnp.where(to_right, column_pick(delta[(0, 1)]), column_pick(delta[(0, -1)])), 1
    )
    k, i = iota((16, 256), 0), iota((16, 256), 1)
    column_place = twice(
        jnp.where((k < 3) & (i == k + 253), 1.0, 0.0)
        + jnp.where((k >= 8) & (k < 11) & (i == cols + k - 8), 1.0, 0.0),
        0,
    )
    k, i = iota((8, 256), 0), iota((8, 256), 1)
    line_pick = twice(
        jnp.where(((k == 2) & (i == 0)) | ((k == 3) & (i == cols)), 1.0, 0.0), 1
    )
    i, j = iota((256, COLS), 0), iota((256, COLS), 1)
    line_map = jnp.concatenate(
        [
            twice(jnp.where(i == 2 * j, 1.0, 0.0), 0),
            twice(jnp.where(i >= 0, 1.0, 0.0), 0),
        ],
        axis=0,
    )
    k, i = iota((8, COLS), 0), iota((8, COLS), 1)
    line_place = twice(
        jnp.where(((k == 0) & (i == 0)) | ((k == 1) & (i == cols)), 1.0, 0.0), 0
    )

    sub8, lane8 = iota((8, COLS), 0), iota((8, COLS), 1)
    odd_lane = (lane8 & 1) == 1
    upper8 = sub8 >= 4
    inside8 = lane8 < cols
    row40, lane40 = iota((40, 256), 0), iota((40, 256), 1)
    corner_ok = (row40 <= rows) & (lane40 <= cols)
    row32, lane32 = iota((ROWS, COLS), 0), iota((ROWS, COLS), 1)
    cell_ok = (row32 < rows) & (lane32 < cols)

    pl.semaphore_wait(barrier, len(AROUND))

    copies = []

    def send(section, index, source, target):
        copy = pltpu.make_async_remote_copy(
            src_ref=source,
            dst_ref=target,
            send_sem=send_sem.at[section, index],
            recv_sem=recv_sem.at[section, index],
            device_id=places[index % 8],
            device_id_type=MESH,
        )
        copy.start()
        copies.append(copy)
        return copy

    for section in range(2):
        if section == 0:
            state = [jnp.where(cell_ok, fields[c], 0.0) for c in range(7)]
        else:
            state = [current[c] for c in range(7)]

        halo = []
        for k, offset in enumerate(AROUND[6:]):
            if k == 0:
                stacked = jnp.concatenate(state + [jnp.zeros((ROWS, COLS), F32)], axis=0)
                columns = dot(column_map, halves(stacked, 1), ((1,), (1,)))
                lane = iota((8, 256), 1) >> 5
            part = columns[8 * k : 8 * k + 8]
            part = jnp.where(lane == 5, roll(part, -3, 0), part)
            col_out[section, k] = dot(halves(part, 1), row_maps[k])
            halo.append(
                send(section, 6 + k, col_out.at[section, k], col_in.at[section, k])
            )
        for upper in (True, False):
            if upper:
                block = [
                    pick(level, (v[0:8], v[8:16], v[24:32])) for v in state
                ]
            else:
                block = [v[0:8] for v in state]
            choices = strip_choices(block, upper, sub8, odd_lane)
            for k in range(0, 3) if upper else range(3, 6):
                d = delta[AROUND[k]]
                chosen = [
                    jnp.where(d == 0, a, jnp.where(d < 0, b, c)) for a, b, c in zip(*choices)
                ]
                chosen.append(jnp.zeros((8, COLS), F32))
                packed = [
                    jnp.where(upper8 == upper, chosen[2 * m], roll(chosen[2 * m + 1], 4, 0))
                    for m in range(4)
                ]
                packed = jnp.concatenate(packed, axis=0)
                row_out[section, k] = dot(halves(packed, 1), lane_maps[k])
                halo.append(send(section, k, row_out.at[section, k], row_in.at[section, k]))
        for copy in halo:
            copy.wait_recv()

        received = jnp.concatenate([col_in[section, 1], col_in[section, 0]], axis=0)
        sides = dot(halves(received, 0), column_place, ((0,), (0,)))
        for c in range(7):
            def strip(k):
                block = row_in[section, k, 8 * (c // 2) : 8 * (c // 2) + 8]
                return roll(block, 4, 0) if c % 2 else block

            low = [
                jnp.where(inside8, strip(0), strip(2)),
                jnp.where(lane8 < 64, strip(2), strip(1)),
            ]
            high = [
                jnp.where(inside8, strip(3), strip(5)),
                jnp.where(lane8 < 64, strip(5), strip(4)),
            ]
            for h in range(2):
                lanes = slice(128 * h, 128 * h + 128)
                for b in range(4):
                    block = sides[32 * c + 8 * b : 32 * c + 8 * b + 8, lanes]
                    if h == 0:
                        block = jnp.where(inside8, state[c][8 * b : 8 * b + 8], block)
                    if b in (1, 2):
                        block = jnp.where(level == b - 1, high[h], block)
                    ghosted[c, 8 * b : 8 * b + 8, lanes] = block
                ghosted[c, 32:40, lanes] = jnp.where(upper8, low[h], high[h])

        density = ghosted[0]
        inverse = 1.0 / density
        speed_x, speed_y, speed_z = (ghosted[c] * inverse for c in (1, 2, 3))
        field_z, face_x, face_y = ghosted[4], ghosted[5], ghosted[6]
        centre_x = 0.5 * (face_x + roll(face_x, -1, 1))
        centre_y = 0.5 * (face_y + roll(face_y, -1, 0))
        flux_x = sweep([density, speed_x, speed_y, speed_z, centre_y, field_z], face_x, 1)
        flux_y = sweep([density, speed_y, speed_x, speed_z, centre_x, field_z], face_y, 0)
        edge = 0.25 * (
            (flux_y[4] + roll(flux_y[4], 1, 1)) - (flux_x[4] + roll(flux_x[4], 1, 0))
        )
        edge = jnp.where(corner_ok, edge, 0.0)

        tall = jnp.concatenate([edge, jnp.zeros((88, 256), F32)], axis=0)
        lines = dot(line_pick, halves(tall, 1), ((1,), (1,)))
        lines = jnp.concatenate([lines, jnp.zeros((8, 128), F32)], axis=1)
        k, i = iota((8, 256), 0), iota((8, 256), 1)
        first_row = edge[0:1]
        last_row = pick(level, (edge[8:9], edge[16:17], edge[32:33]))
        lines = jnp.where(k == 0, first_row, jnp.where(k == 1, last_row, lines))
        ends = jnp.where(k < 6, first_row, last_row)
        ends = jnp.where((k >= 4) & (i == jnp.where((k & 1) == 0, 0, cols)), ends, 0.0)
        line_out[section] = dot(
            jnp.concatenate([halves(lines, 1), halves(ends, 1)], axis=1), line_map
        )
        shared = [
            send(section, 8 + k, line_out.at[section], line_in.at[section, k])
            for k in range(8)
        ]

        change = [
            (roll(flux_x[a], -1, 1) - flux_x[a]) + (roll(flux_y[b], -1, 0) - flux_y[b])
            for a, b in ((0, 0), (1, 2), (2, 1), (3, 3), (5, 5))
        ]

        def finish(c, value):
            if section == 0:
                current[c] = jnp.where(cell_ok, value, 0.0)
            else:
                out[c] = jnp.where(cell_ok, 0.5 * (fields[c] + value), 0.0)

        for c in range(5):
            finish(c, state[c] - ratio * change[c][:ROWS, :COLS])

        for copy in shared:
            copy.wait_recv()

        def border(offset):
            back = AROUND.index((-offset[0], -offset[1]))
            return line_in[section, back], near[offset] > level

        below, w_below = border((-1, 0))
        above, w_above = border((1, 0))
        left, w_left = border((0, -1))
        right, w_right = border((0, 1))
        sides = jnp.where(
            sub8 == 0, left[3:4], jnp.where(sub8 == 1, right[2:3], 0.0)
        )
        sides = dot(halves(sides, 0), line_place, ((0,), (0,)))[:24]
        row24, lane24 = iota((24, COLS), 0), iota((24, COLS), 1)
        part = edge[:24, :COLS]
        on_low, on_high = row24 == 0, row24 == rows
        on_left, on_right = lane24 == 0, lane24 == cols

        def flag(condition):
            return jnp.where(condition, 1.0, 0.0).astype(F32)

        part = jnp.where(on_low, flag(w_below) * below[1:2] + (1.0 - flag(w_below)) * part, part)
        part = jnp.where(on_high, flag(w_above) * above[0:1] + (1.0 - flag(w_above)) * part, part)
        part = jnp.where(on_left, flag(w_left) * sides + (1.0 - flag(w_left)) * part, part)
        part = jnp.where(on_right, flag(w_right) * sides + (1.0 - flag(w_right)) * part, part)
        for vertical, beside, horizontal, v_row, h_row, offset in (
            ((below, w_below), (left, w_left), (on_low, on_left), 6, 5, (-1, -1)),
            ((below, w_below), (right, w_right), (on_low, on_right), 7, 4, (-1, 1)),
            ((above, w_above), (left, w_left), (on_high, on_left), 4, 7, (1, -1)),
            ((above, w_above), (right, w_right), (on_high, on_right), 5, 6, (1, 1)),
        ):
            far, w_far = border(offset)
            d_row = 11 - (4 + (2 if offset[0] > 0 else 0) + (1 if offset[1] > 0 else 0))
            a, b, c = flag(vertical[1]), flag(beside[1]), flag(w_far)
            count = a + b + c
            share = jnp.where(count > 2.5, jnp.float32(1.0 / 3.0), jnp.where(count > 1.5, 0.5, 1.0))
            value = share * (
                a * vertical[0][v_row : v_row + 1]
                + b * beside[0][h_row : h_row + 1]
                + c * far[d_row + 0 : d_row + 1]
            )
            keep = flag(count < 0.5)
            part = jnp.where(
                horizontal[0] & horizontal[1], keep * edge[:24, :COLS] + (1.0 - keep) * value, part
            )
        top = jnp.concatenate([part, edge[:24, COLS:]], axis=1)
        edge = jnp.concatenate([top, edge[24:]], axis=0)
        finish(5, state[5] - ratio * (roll(edge, -1, 0) - edge)[:ROWS, :COLS])
        finish(6, state[6] + ratio * (roll(edge, -1, 1) - edge)[:ROWS, :COLS])

    for copy in copies:
        copy.wait_send()


def on_device(seg_count, sub_count, fields, region_levels):
    vmem = pl.BlockSpec(memory_space=pltpu.VMEM)
    return pl.pallas_call(
        functools.partial(kernel, seg_count, sub_count),
        out_shape=jax.ShapeDtypeStruct(fields.shape, F32),
        in_specs=[vmem, pl.BlockSpec(memory_space=pltpu.SMEM)],
        out_specs=vmem,
        scratch_shapes=[
            pltpu.VMEM((7, 40, 256), F32),
            pltpu.VMEM((7, ROWS, COLS), F32),
            pltpu.VMEM((2, 6, 32, COLS), F32),
            pltpu.VMEM((2, 6, 32, COLS), F32),
            pltpu.VMEM((2, 2, 8, 256), F32),
            pltpu.VMEM((2, 2, 8, 256), F32),
            pltpu.VMEM((2, 8, COLS), F32),
            pltpu.VMEM((2, 8, 8, COLS), F32),
            pltpu.VMEM((6, 256, COLS), BF16),
            pltpu.VMEM((2, 512, 256), BF16),
            pltpu.SemaphoreType.DMA((2, 16)),
            pltpu.SemaphoreType.DMA((2, 16)),
        ],
        compiler_params=pltpu.CompilerParams(
            collective_id=0, has_side_effects=True, vmem_limit_bytes=32 * 1024 * 1024
        ),
    )(fields, region_levels)


def solution(mesh):
    body = functools.partial(on_device, mesh.shape["seg"], mesh.shape["sub"])
    return jax.shard_map(
        body,
        mesh=mesh,
        in_specs=(P(None, "seg", "sub"), P()),
        out_specs=P(None, "seg", "sub"),
        check_vma=False,
    )
```

profile of v0, /device:TPU:0, one launch (start us, length us, event | category | flops | bytes accessed | tf_op | source)
XLA Modules:
  0.0 30.7 jit_solution(15998187443613700704)
XLA Ops:
  0.0 0.8 %copy.3.levels = s32[8,4]{1,0:T(8,128)S(1)} copy(s32[8,4]{0,1:T(4,128)} %param.3) | data formatting | bytes 256 | tf_op args[1]
  0.8 0.0 copy-start
  0.8 0.9 %copy-done = f32[7,32,128]{2,1,0:T(8,128)S(1)} copy-done((f32[7,32,128]{2,1,0:T(8,128)S(1)}, f32[7,32,128]{2,1,0:T(8,128)}, u32[]{:S(2)}) %copy-start) | copy-done | bytes 114712
  1.7 28.4 %shard_map.28 = f32[7,32,128]{2,1,0:T(8,128)S(1)} custom-call(f32[7,32,128]{2,1,0:T(8,128)S(1)} %copy-done, s32[8,4]{1,0:T(8,128)S(1)} %copy.3.levels), custom_call_target="tpu_custom_call" | custom-call | tf_op jit(solution)/shard_map/pallas_call | solution.py:387
  30.1 0.6 %copy.5 = f32[7,32,128]{2,1,0:T(8,128)} copy(f32[7,32,128]{2,1,0:T(8,128)S(1)} %shard_map.28) | data formatting | bytes 229376
Async XLA Ops:
  0.8 0.9 %copy-start = (f32[7,32,128]{2,1,0:T(8,128)S(1)}, f32[7,32,128]{2,1,0:T(8,128)}, u32[]{:S(2)}) copy-start(f32[7,32,128]{2,1,0:T(8,128)} %fields.1) | copy-start | bytes 344068
where the time goes:
time: 30.9 us; the launch traced here: 30.7 us
  Pallas kernels  28.4 us (92%)
  local copies, waits for them, and re-layouts  2.3 us (7%)
    pallas_call x1, Pallas kernels, on_device(): pl.pallas_call(functools.partial(kernel, seg_count, sub_count), out_shape...  28.4 us
    unnamed x4, local copies, waits for them, and re-layouts  2.3 us

commit v1 on v0

--- a/solution.py
+++ b/solution.py
@@ -107,10 +107,16 @@
 
 
 def kernel(
-    seg_count, sub_count, fields, levels, out,
-    ghosted, current, row_out, row_in, col_out, col_in, line_out, line_in,
-    lane_maps, row_maps, send_sem, recv_sem,
+    seg_count, sub_count, fields_hbm, levels_hbm, out,
+    fields, levels, ghosted, current, row_out, row_in, col_out, col_in, line_out, line_in,
+    lane_maps, row_maps, send_sem, recv_sem, fetch_sem,
 ):
+    fetches = [
+        pltpu.make_async_copy(levels_hbm, levels, fetch_sem.at[0]),
+        pltpu.make_async_copy(fields_hbm, fields, fetch_sem.at[1]),
+    ]
+    for fetch in fetches:
+        fetch.start()
     seg, sub = lax.axis_index("seg"), lax.axis_index("sub")
 
     def place(offset):
@@ -124,8 +130,9 @@
     for target in places:
         pl.semaphore_signal(barrier, inc=1, device_id=target, device_id_type=MESH)
 
-    level = levels[seg, sub]
-    near = {offset: levels[p[0], p[1]] for offset, p in zip(AROUND, places)}
+    fetches[0].wait()
+    level = levels[sub, seg]
+    near = {offset: levels[p[1], p[0]] for offset, p in zip(AROUND, places)}
     rows = pick(level, (8, 16, 32))
     cols = pick(level, (32, 64, 128))
     ratio = pick(level, [jnp.float32(STEP_SIZE / h) for h in (4.0, 2.0, 1.0)])
@@ -197,8 +204,7 @@
     row32, lane32 = iota((ROWS, COLS), 0), iota((ROWS, COLS), 1)
     cell_ok = (row32 < rows) & (lane32 < cols)
 
-    pl.semaphore_wait(barrier, len(AROUND))
-
+    fetches[1].wait()
     copies = []
 
     def send(section, index, source, target):
@@ -229,9 +235,6 @@
             part = columns[8 * k : 8 * k + 8]
             part = jnp.where(lane == 5, roll(part, -3, 0), part)
             col_out[section, k] = dot(halves(part, 1), row_maps[k])
-            halo.append(
-                send(section, 6 + k, col_out.at[section, k], col_in.at[section, k])
-            )
         for upper in (True, False):
             if upper:
                 block = [
@@ -252,7 +255,12 @@
                 ]
                 packed = jnp.concatenate(packed, axis=0)
                 row_out[section, k] = dot(halves(packed, 1), lane_maps[k])
-                halo.append(send(section, k, row_out.at[section, k], row_in.at[section, k]))
+        if section == 0:
+            pl.semaphore_wait(barrier, len(AROUND))
+        for k in range(2):
+            halo.append(send(section, 6 + k, col_out.at[section, k], col_in.at[section, k]))
+        for k in range(6):
+            halo.append(send(section, k, row_out.at[section, k], row_in.at[section, k]))
         for copy in halo:
             copy.wait_recv()
 
@@ -384,12 +392,17 @@
 
 def on_device(seg_count, sub_count, fields, region_levels):
     vmem = pl.BlockSpec(memory_space=pltpu.VMEM)
+    region_levels = region_levels.T
+    fields = pltpu.with_memory_space_constraint(fields, pltpu.HBM)
+    region_levels = pltpu.with_memory_space_constraint(region_levels, pltpu.HBM)
     return pl.pallas_call(
         functools.partial(kernel, seg_count, sub_count),
         out_shape=jax.ShapeDtypeStruct(fields.shape, F32),
-        in_specs=[vmem, pl.BlockSpec(memory_space=pltpu.SMEM)],
+        in_specs=[pl.BlockSpec(memory_space=pltpu.HBM)] * 2,
         out_specs=vmem,
         scratch_shapes=[
+            pltpu.VMEM(fields.shape, F32),
+            pltpu.SMEM(region_levels.shape, I32),
             pltpu.VMEM((7, 40, 256), F32),
             pltpu.VMEM((7, ROWS, COLS), F32),
             pltpu.VMEM((2, 6, 32, COLS), F32),
@@ -402,6 +415,7 @@
             pltpu.VMEM((2, 512, 256), BF16),
             pltpu.SemaphoreType.DMA((2, 16)),
             pltpu.SemaphoreType.DMA((2, 16)),
+            pltpu.SemaphoreType.DMA((2,)),
         ],
         compiler_params=pltpu.CompilerParams(
             collective_id=0, has_side_effects=True, vmem_limit_bytes=32 * 1024 * 1024

time: 30.9 us -> 28 us (0.906)
  local copies, waits for them, and re-layouts: 2.3 us -> 0.65 us
  Pallas kernels: 28.4 us -> 27.2 us
    unnamed x4 -> x1, local copies, waits for them, and re-layouts: 2.3 us -> 0.65 us
    pallas_call x1, Pallas kernels: 28.4 us -> 27.2 us  [on_device(): pl.pallas_call(functools.partial(kernel, seg_count, sub_count), out_shape...]
where the time goes in v1:
time: 28 us; the launch traced here: 27.8 us
  Pallas kernels  27.2 us (97%)
  local copies, waits for them, and re-layouts  0.65 us (2%)
    pallas_call x1, Pallas kernels, on_device(): pl.pallas_call(functools.partial(kernel, seg_count, sub_count), out_shape...  27.2 us
    unnamed x1, local copies, waits for them, and re-layouts  0.65 us

profile of v1, /device:TPU:0, one launch (start us, length us, event | category | flops | bytes accessed | tf_op | source)
XLA Modules:
  0.0 27.8 jit_solution(3188427585540973433)
XLA Ops:
  0.0 27.2 %shard_map.28 = f32[7,32,128]{2,1,0:T(8,128)S(1)} custom-call(f32[7,32,128]{2,1,0:T(8,128)} %fields_hbm.1, s32[4,8]{1,0:T(4,128)} %bitcast.1), custom_call_target="tpu_custom_call" | custom-call | tf_op jit(solution)/shard_map/pallas_call | solution.py:398
  27.2 0.6 %copy.4 = f32[7,32,128]{2,1,0:T(8,128)} copy(f32[7,32,128]{2,1,0:T(8,128)S(1)} %shard_map.28) | data formatting | bytes 229376

commit v2 on v1

--- a/solution.py
+++ b/solution.py
@@ -108,7 +108,7 @@
 
 def kernel(
     seg_count, sub_count, fields_hbm, levels_hbm, out,
-    fields, levels, ghosted, current, row_out, row_in, col_out, col_in, line_out, line_in,
+    fields, levels, ghosted, current, row_out, row_in, corner_out, corner_in, col_out, col_in, line_out, line_in,
     lane_maps, row_maps, send_sem, recv_sem, fetch_sem,
 ):
     fetches = [
@@ -234,7 +234,8 @@
                 lane = iota((8, 256), 1) >> 5
             part = columns[8 * k : 8 * k + 8]
             part = jnp.where(lane == 5, roll(part, -3, 0), part)
-            col_out[section, k] = dot(halves(part, 1), row_maps[k])
+            part = dot(halves(part, 1), row_maps[k])
+            col_out[section, k] = jnp.where(upper8, roll(part[:, COLS:], 4, 0), part[:, :COLS])
         for upper in (True, False):
             if upper:
                 block = [
@@ -254,21 +255,41 @@
                     for m in range(4)
                 ]
                 packed = jnp.concatenate(packed, axis=0)
-                row_out[section, k] = dot(halves(packed, 1), lane_maps[k])
+                packed = dot(halves(packed, 1), lane_maps[k])
+                if k % 3 == 0:
+                    row_out[section, k // 3] = packed
+                else:
+                    corner = packed[0:8]
+                    for m in range(1, 4):
+                        corner = corner + roll(packed[8 * m : 8 * m + 8], 32 * m, 1)
+                    corner_out[section, k] = corner
         if section == 0:
             pl.semaphore_wait(barrier, len(AROUND))
         for k in range(2):
             halo.append(send(section, 6 + k, col_out.at[section, k], col_in.at[section, k]))
-        for k in range(6):
-            halo.append(send(section, k, row_out.at[section, k], row_in.at[section, k]))
+        for k in (1, 2, 4, 5):
+            halo.append(send(section, k, corner_out.at[section, k], corner_in.at[section, k]))
+        for k in (0, 3):
+            halo.append(
+                send(section, k, row_out.at[section, k // 3], row_in.at[section, k // 3])
+            )
         for copy in halo:
             copy.wait_recv()
 
-        received = jnp.concatenate([col_in[section, 1], col_in[section, 0]], axis=0)
+        received = jnp.concatenate(
+            [
+                jnp.concatenate([part, roll(part, 4, 0)], axis=1)
+                for part in (col_in[section, 1], col_in[section, 0])
+            ],
+            axis=0,
+        )
         sides = dot(halves(received, 0), column_place, ((0,), (0,)))
         for c in range(7):
             def strip(k):
-                block = row_in[section, k, 8 * (c // 2) : 8 * (c // 2) + 8]
+                if k % 3 == 0:
+                    block = row_in[section, k // 3, 8 * (c // 2) : 8 * (c // 2) + 8]
+                else:
+                    block = roll(corner_in[section, k], -32 * (c // 2), 1)
                 return roll(block, 4, 0) if c % 2 else block
 
             low = [
@@ -405,10 +426,12 @@
             pltpu.SMEM(region_levels.shape, I32),
             pltpu.VMEM((7, 40, 256), F32),
             pltpu.VMEM((7, ROWS, COLS), F32),
-            pltpu.VMEM((2, 6, 32, COLS), F32),
-            pltpu.VMEM((2, 6, 32, COLS), F32),
-            pltpu.VMEM((2, 2, 8, 256), F32),
-            pltpu.VMEM((2, 2, 8, 256), F32),
+            pltpu.VMEM((2, 2, 32, COLS), F32),
+            pltpu.VMEM((2, 2, 32, COLS), F32),
+            pltpu.VMEM((2, 6, 8, COLS), F32),
+            pltpu.VMEM((2, 6, 8, COLS), F32),
+            pltpu.VMEM((2, 2, 8, COLS), F32),
+            pltpu.VMEM((2, 2, 8, COLS), F32),
             pltpu.VMEM((2, 8, COLS), F32),
             pltpu.VMEM((2, 8, 8, COLS), F32),
             pltpu.VMEM((6, 256, COLS), BF16),

time: 28 us -> 26.9 us (0.961)
  Pallas kernels: 27.2 us -> 26.1 us
    pallas_call x1, Pallas kernels: 27.2 us -> 26.1 us  [on_device(): pl.pallas_call(functools.partial(kernel, seg_count, sub_count), out_shape...]
where the time goes in v2:
time: 26.9 us; the launch traced here: 26.7 us
  Pallas kernels  26.1 us (97%)
  local copies, waits for them, and re-layouts  0.65 us (2%)
    pallas_call x1, Pallas kernels, on_device(): pl.pallas_call(functools.partial(kernel, seg_count, sub_count), out_shape...  26.1 us
    unnamed x1, local copies, waits for them, and re-layouts  0.65 us

profile of v2, /device:TPU:0, one launch (start us, length us, event | category | flops | bytes accessed | tf_op | source)
XLA Modules:
  0.0 26.7 jit_solution(6770104231223076522)
XLA Ops:
  0.0 26.1 %shard_map.28 = f32[7,32,128]{2,1,0:T(8,128)S(1)} custom-call(f32[7,32,128]{2,1,0:T(8,128)} %fields_hbm.1, s32[4,8]{1,0:T(4,128)} %bitcast.1), custom_call_target="tpu_custom_call" | custom-call | tf_op jit(solution)/shard_map/pallas_call | solution.py:419
  26.1 0.6 %copy.4 = f32[7,32,128]{2,1,0:T(8,128)} copy(f32[7,32,128]{2,1,0:T(8,128)S(1)} %shard_map.28) | data formatting | bytes 229376

commit v3 on v2

--- a/solution.py
+++ b/solution.py
@@ -220,11 +220,14 @@
         copies.append(copy)
         return copy
 
-    for section in range(2):
-        if section == 0:
-            state = [jnp.where(cell_ok, fields[c], 0.0) for c in range(7)]
-        else:
-            state = [current[c] for c in range(7)]
+    for c in range(7):
+        current[c] = jnp.where(cell_ok, fields[c], 0.0)
+
+    @pl.loop(0, 2)
+    def _(section):
+        copies.clear()
+        state = [current[c] for c in range(7)]
+        last = section == 1
 
         halo = []
         for k, offset in enumerate(AROUND[6:]):
@@ -263,8 +266,11 @@
                     for m in range(1, 4):
                         corner = corner + roll(packed[8 * m : 8 * m + 8], 32 * m, 1)
                     corner_out[section, k] = corner
-        if section == 0:
+
+        @pl.when(section == 0)
+        def _():
             pl.semaphore_wait(barrier, len(AROUND))
+
         for k in range(2):
             halo.append(send(section, 6 + k, col_out.at[section, k], col_in.at[section, k]))
         for k in (1, 2, 4, 5):
@@ -347,10 +353,8 @@
         ]
 
         def finish(c, value):
-            if section == 0:
-                current[c] = jnp.where(cell_ok, value, 0.0)
-            else:
-                out[c] = jnp.where(cell_ok, 0.5 * (fields[c] + value), 0.0)
+            value = jnp.where(last, 0.5 * (fields[c] + value), value)
+            current[c] = jnp.where(cell_ok, value, 0.0)
 
         for c in range(5):
             finish(c, state[c] - ratio * change[c][:ROWS, :COLS])
@@ -407,8 +411,11 @@
         finish(5, state[5] - ratio * (roll(edge, -1, 0) - edge)[:ROWS, :COLS])
         finish(6, state[6] + ratio * (roll(edge, -1, 1) - edge)[:ROWS, :COLS])
 
-    for copy in copies:
-        copy.wait_send()
+        for copy in copies:
+            copy.wait_send()
+
+    for c in range(7):
+        out[c] = current[c]
 
 
 def on_device(seg_count, sub_count, fields, region_levels):

time: 26.9 us -> 27 us (level)
  no operation moved by 1% of the time
where the time goes in v3:
time: 27 us; the launch traced here: 26.8 us
  Pallas kernels  26.1 us (97%)
  local copies, waits for them, and re-layouts  0.65 us (2%)
    pallas_call x1, Pallas kernels, on_device(): pl.pallas_call(functools.partial(kernel, seg_count, sub_count), out_shape...  26.1 us
    unnamed x1, local copies, waits for them, and re-layouts  0.65 us

profile of v3, /device:TPU:0, one launch (start us, length us, event | category | flops | bytes accessed | tf_op | source)
XLA Modules:
  0.0 26.8 jit_solution(396696307006869732)
XLA Ops:
  0.0 26.1 %shard_map.28 = f32[7,32,128]{2,1,0:T(8,128)S(1)} custom-call(f32[7,32,128]{2,1,0:T(8,128)} %fields_hbm.1, s32[4,8]{1,0:T(4,128)} %bitcast.1), custom_call_target="tpu_custom_call" | custom-call | tf_op jit(solution)/shard_map/pallas_call | solution.py:426
  26.2 0.6 %copy.4 = f32[7,32,128]{2,1,0:T(8,128)} copy(f32[7,32,128]{2,1,0:T(8,128)S(1)} %shard_map.28) | data formatting | bytes 229376

commit v4 on v2

--- a/solution.py
+++ b/solution.py
@@ -54,31 +54,43 @@
 def sweep(primitives, normal, axis):
     left, right = [], []
     for value in primitives:
+        if value is None:
+            left.append(None)
+            right.append(None)
+            continue
         before = value - roll(value, 1, axis)
         half = 0.5 * minmod(before, roll(before, -1, axis))
         left.append(roll(value + half, 1, axis))
         right.append(value - half)
 
+    return riemann(left, right, normal)
+
+
+def riemann(left, right, normal):
     def pieces(values):
         density, speed_n, speed_t, speed_z, field_t, field_z = values
         square = normal * normal + field_t * field_t + field_z * field_z
         moment = density * speed_n
-        cons = [density, moment, density * speed_t, density * speed_z, field_t, field_z]
+        cons = [density, moment, density * speed_t, None, field_t, field_z]
         flux = [
             moment,
             moment * speed_n + (density + 0.5 * square) - normal * normal,
             moment * speed_t - normal * field_t,
-            moment * speed_z - normal * field_z,
+            None,
             field_t * speed_n - normal * speed_t,
-            field_z * speed_n - normal * speed_z,
+            None,
         ]
+        if speed_z is not None:
+            cons[3] = density * speed_z
+            flux[3] = moment * speed_z - normal * field_z
+            flux[5] = field_z * speed_n - normal * speed_z
         return flux, cons, jnp.abs(speed_n) + jnp.sqrt(1.0 + square / density)
 
     flux_l, cons_l, signal_l = pieces(left)
     flux_r, cons_r, signal_r = pieces(right)
     fastest = jnp.maximum(signal_l, signal_r)
     return [
-        0.5 * ((fl + fr) - fastest * (cr - cl))
+        None if fl is None else 0.5 * ((fl + fr) - fastest * (cr - cl))
         for fl, fr, cl, cr in zip(flux_l, flux_r, cons_l, cons_r)
     ]
 
@@ -108,8 +120,8 @@
 
 def kernel(
     seg_count, sub_count, fields_hbm, levels_hbm, out,
-    fields, levels, ghosted, current, row_out, row_in, corner_out, corner_in, col_out, col_in, line_out, line_in,
-    lane_maps, row_maps, send_sem, recv_sem, fetch_sem,
+    fields, levels, ghosted, current, row_out, row_in, corner_out, corner_in, col_out, col_in,
+    lane_maps, row_maps, fine_map, send_sem, recv_sem, fetch_sem,
 ):
     fetches = [
         pltpu.make_async_copy(levels_hbm, levels, fetch_sem.at[0]),
@@ -158,6 +170,8 @@
         faces = jnp.where(d < 0, jnp.where(i == 2 * j, 1.0, 0.0), resample(i, j, d))
         matrix = jnp.where(together, jnp.where(face_rows, faces, resample(i, j, d)), 0.0)
         row_maps[k] = twice(matrix, 0)
+    source = (i >> 1) + ((i & 1) << 4)
+    fine_map[...] = twice(jnp.where(together, jnp.where(source == j, 1.0, 0.0), 0.0), 0)
     k, i = iota((16, COLS), 0), iota((16, COLS), 1)
     to_right = k >= 8
     k = k & 7
@@ -169,8 +183,15 @@
         faces = jnp.where(d < 0, jnp.where(i == 2 * k, 1.0, 0.0), resample(i, k, d))
         return jnp.where(is_face, faces, resample(i, k, d))
 
+    raw = jnp.where(i == jnp.where(to_right, k - 2, k - 3), 1.0, 0.0)
+    is_raw = (iota((16, COLS), 0) & 7) >= 6
     column_map = twice(
-        jnp.where(to_right, column_pick(delta[(0, 1)]), column_pick(delta[(0, -1)])), 1
+        jnp.where(
+            is_raw,
+            raw,
+            jnp.where(to_right, column_pick(delta[(0, 1)]), column_pick(delta[(0, -1)])),
+        ),
+        1,
     )
     k, i = iota((16, 256), 0), iota((16, 256), 1)
     column_place = twice(
@@ -178,17 +199,18 @@
         + jnp.where((k >= 8) & (k < 11) & (i == cols + k - 8), 1.0, 0.0),
         0,
     )
-    k, i = iota((8, 256), 0), iota((8, 256), 1)
-    line_pick = twice(
-        jnp.where(((k == 2) & (i == 0)) | ((k == 3) & (i == cols)), 1.0, 0.0), 1
-    )
-    i, j = iota((256, COLS), 0), iota((256, COLS), 1)
-    line_map = jnp.concatenate(
-        [
-            twice(jnp.where(i == 2 * j, 1.0, 0.0), 0),
-            twice(jnp.where(i >= 0, 1.0, 0.0), 0),
-        ],
-        axis=0,
+    i, j = iota((COLS, COLS), 0), iota((COLS, COLS), 1)
+    end = jnp.where(j == 8, 0, jnp.where(j == 9, 1, 2 * COLS))
+    border_map = twice(
+        jnp.concatenate(
+            [
+                jnp.where((i >> 1) + ((i & 1) << 6) == j, 1.0, 0.0),
+                jnp.where(i == end + cols - 2, 1.0, 0.0),
+                jnp.where(i == end, 1.0, 0.0),
+            ],
+            axis=1,
+        ),
+        0,
     )
     k, i = iota((8, COLS), 0), iota((8, COLS), 1)
     line_place = twice(
@@ -199,6 +221,22 @@
     odd_lane = (lane8 & 1) == 1
     upper8 = sub8 >= 4
     inside8 = lane8 < cols
+    in_side = (lane8 >= 80) & (lane8 < 96)
+
+    def flag(condition):
+        return jnp.where(condition, 1.0, 0.0).astype(F32)
+
+    finer = {offset: flag(near[offset] > level) for offset in AROUND}
+
+    def by_sublane(low, middle, high):
+        return jnp.where(sub8 < 2, low, jnp.where(sub8 < 6, middle, high))
+
+    finer_left = by_sublane(finer[(-1, -1)], finer[(0, -1)], finer[(1, -1)])
+    finer_right = by_sublane(finer[(-1, 1)], finer[(0, 1)], finer[(1, 1)])
+    finer_rows = by_sublane(finer[(-1, 0)], 0.0, finer[(1, 0)])
+    use_left = jnp.where(lane8 == COLS - 1, finer_left, 0.0) > 0.5
+    use_right = jnp.where(lane8 == cols, finer_right, 0.0) > 0.5
+    use_rows = jnp.where(inside8, finer_rows, 0.0) > 0.5
     row40, lane40 = iota((40, 256), 0), iota((40, 256), 1)
     corner_ok = (row40 <= rows) & (lane40 <= cols)
     row32, lane32 = iota((ROWS, COLS), 0), iota((ROWS, COLS), 1)
@@ -233,9 +271,47 @@
                 columns = dot(column_map, halves(stacked, 1), ((1,), (1,)))
                 lane = iota((8, 256), 1) >> 5
             part = columns[8 * k : 8 * k + 8]
+            fine = dot(halves(part, 1), fine_map[...])
+            col_out[section, k, 8:16] = jnp.where(
+                upper8, fine[:, :COLS], roll(fine[:, COLS:], 4, 0)
+            )
             part = jnp.where(lane == 5, roll(part, -3, 0), part)
             part = dot(halves(part, 1), row_maps[k])
-            col_out[section, k] = jnp.where(upper8, roll(part[:, COLS:], 4, 0), part[:, :COLS])
+            col_out[section, k, 0:8] = jnp.where(
+                upper8, roll(part[:, COLS:], 4, 0), part[:, :COLS]
+            )
+        border = []
+        for v in state:
+            top = pick(level, (v[0:8], v[8:16], v[24:32]))
+            border.append(
+                jnp.where(
+                    sub8 < 2,
+                    roll(top, 2, 0),
+                    jnp.where(
+                        sub8 < 4,
+                        roll(v[0:8], 2, 0),
+                        jnp.where(sub8 < 6, roll(top, 6, 0), roll(v[0:8], 6, 0)),
+                    ),
+                )
+            )
+        border = dot(halves(jnp.concatenate(border, axis=0), 1), border_map)
+        ends = []
+        for part in (border[:, COLS : 2 * COLS], border[:, 2 * COLS :]):
+            total = part[0:8]
+            for c in range(1, 7):
+                total = total + roll(part[8 * c : 8 * c + 8], 16 * c, 1)
+            ends.append(total)
+        col_out[section, 0, 16:24] = ends[1]
+        col_out[section, 1, 16:24] = ends[0]
+        for group in range(2):
+            up = down = jnp.zeros((8, COLS), F32)
+            for q in range(4 if group == 0 else 3):
+                c = 4 * group + q
+                part = roll(border[8 * c : 8 * c + 8, :COLS], 2 * q, 0)
+                up = jnp.where((sub8 >> 1) == q, part, up)
+                down = jnp.where((sub8 >> 1) == ((3 + q) & 3), part, down)
+            row_out[section, 0, 32 + 8 * group : 40 + 8 * group] = up
+            row_out[section, 1, 32 + 8 * group : 40 + 8 * group] = down
         for upper in (True, False):
             if upper:
                 block = [
@@ -257,12 +333,12 @@
                 packed = jnp.concatenate(packed, axis=0)
                 packed = dot(halves(packed, 1), lane_maps[k])
                 if k % 3 == 0:
-                    row_out[section, k // 3] = packed
+                    row_out[section, k // 3, 0:32] = packed
                 else:
                     corner = packed[0:8]
                     for m in range(1, 4):
                         corner = corner + roll(packed[8 * m : 8 * m + 8], 32 * m, 1)
-                    corner_out[section, k] = corner
+                    corner_out[section, k] = corner + ends[0 if k % 3 == 1 else 1]
         if section == 0:
             pl.semaphore_wait(barrier, len(AROUND))
         for k in range(2):
@@ -279,7 +355,7 @@
         received = jnp.concatenate(
             [
                 jnp.concatenate([part, roll(part, 4, 0)], axis=1)
-                for part in (col_in[section, 1], col_in[section, 0])
+                for part in (col_in[section, 1, 0:8], col_in[section, 0, 0:8])
             ],
             axis=0,
         )
@@ -324,22 +400,89 @@
         )
         edge = jnp.where(corner_ok, edge, 0.0)
 
-        tall = jnp.concatenate([edge, jnp.zeros((88, 256), F32)], axis=0)
-        lines = dot(line_pick, halves(tall, 1), ((1,), (1,)))
-        lines = jnp.concatenate([lines, jnp.zeros((8, 128), F32)], axis=1)
-        k, i = iota((8, 256), 0), iota((8, 256), 1)
-        first_row = edge[0:1]
-        last_row = pick(level, (edge[8:9], edge[16:17], edge[32:33]))
-        lines = jnp.where(k == 0, first_row, jnp.where(k == 1, last_row, lines))
-        ends = jnp.where(k < 6, first_row, last_row)
-        ends = jnp.where((k >= 4) & (i == jnp.where((k & 1) == 0, 0, cols)), ends, 0.0)
-        line_out[section] = dot(
-            jnp.concatenate([halves(lines, 1), halves(ends, 1)], axis=1), line_map
-        )
-        shared = [
-            send(section, 8 + k, line_out.at[section], line_in.at[section, k])
-            for k in range(8)
-        ]
+        from_left = by_sublane(
+            corner_in[section, 1], col_in[section, 1, 16:24], corner_in[section, 4]
+        )
+        from_right = by_sublane(
+            corner_in[section, 2], col_in[section, 0, 16:24], corner_in[section, 5]
+        )
+        from_right = jnp.where(level == 0, roll(from_right, 32, 1), roll(from_right, 64, 1))
+        beside = []
+        for k in (1, 0):
+            part = col_in[section, k, 8:16]
+            part = jnp.concatenate([part, roll(part, 4, 0)], axis=1)
+            beside.append(roll(part, 2, 0) if k == 1 else part)
+        own_sides = jnp.where(sub8[:, :1] < 4, columns[6:7], columns[15:16])
+        sub_wide = iota((8, 256), 0)
+
+        def side_window(odd):
+            left, right = (roll(v, -16, 1) if odd else v for v in beside)
+            left = jnp.where(finer[(0, -1)] > 0.5, left, received[2:3])
+            right = jnp.where(finer[(0, 1)] > 0.5, right, received[8:9])
+            return jnp.where(sub_wide < 2, left, jnp.where(sub_wide < 6, own_sides, right))
+
+        side_windows = [side_window(False), side_window(True)]
+        swapped = (0, 2, 1, 3, 4, 6, 5)
+
+        def windows(c):
+            first = jnp.where(lane8 == COLS - 1, ghosted[c, 39:40, COLS:], ghosted[c, 39:40, :COLS])
+            second = jnp.where(lane8 == COLS - 1, ghosted[c, 0:1, COLS:], ghosted[c, 0:1, :COLS])
+
+            def at_level(low, high):
+                value = jnp.where(level == 0, ghosted[c, low : low + 1], ghosted[c, high : high + 1])
+                return jnp.where(lane8 == COLS - 1, value[:, COLS:], value[:, :COLS])
+
+            base = jnp.where(
+                sub8 < 2,
+                first,
+                jnp.where(sub8 < 4, second, jnp.where(sub8 < 6, at_level(7, 15), at_level(8, 16))),
+            )
+            q, rows_of = c % 4, slice(32 + 8 * (c // 4), 40 + 8 * (c // 4))
+            fine = jnp.where(
+                upper8,
+                roll(row_in[section, 1, rows_of], -2 * q, 0),
+                roll(row_in[section, 0, rows_of], -2 * q, 0),
+            )
+            pair = []
+            for odd in range(2):
+                value = jnp.where(use_rows, roll(fine, 64, 1) if odd else fine, base)
+                value = jnp.where(use_left, roll(from_left, 127 - (16 * c + 8 + odd), 1), value)
+                value = jnp.where(use_right, roll(from_right, -(16 * c + 8 + odd), 1), value)
+                t = swapped[c]
+                half = side_windows[odd][:, COLS * (t // 4) : COLS * (t // 4) + COLS]
+                pair.append(jnp.where(in_side, roll(half, 80 - 32 * (t % 4), 1), value))
+            return pair
+
+        even, odd = zip(*[windows(c) if c != 3 else (None, None) for c in range(7)])
+
+        def primitives_of(v):
+            inv = 1.0 / v[0]
+            return v[0], v[1] * inv, v[2] * inv, v[4], v[5], v[6]
+
+        even, odd = primitives_of(even), primitives_of(odd)
+        odd_before = [roll(v, 1, 1) for v in odd]
+        even_before = [roll(v, 1, 1) for v in even]
+
+        def along_rows(v, centre):
+            return sweep([v[0], v[2], v[1], None, centre, v[3]], v[5], 0)[4]
+
+        fine_y = along_rows(even, 0.5 * (even[4] + odd[4])) + along_rows(
+            odd_before, 0.5 * (odd_before[4] + even[4])
+        )
+
+        def across(v):
+            centre = 0.5 * (v[5] + roll(v[5], -1, 0))
+            return [v[0], v[1], v[2], centre, v[3]]
+
+        left, right = [], []
+        for a, b, c, d in zip(*[across(v) for v in (even_before, odd_before, even, odd)]):
+            middle = c - b
+            left.append(b + 0.5 * minmod(b - a, middle))
+            right.append(c - 0.5 * minmod(middle, d - c))
+        left.insert(3, None)
+        right.insert(3, None)
+        fine_x = riemann(left, right, even[4])[4]
+        fine_edge = 0.25 * (fine_y - (fine_x + roll(fine_x, 1, 0)))
 
         change = [
             (roll(flux_x[a], -1, 1) - flux_x[a]) + (roll(flux_y[b], -1, 0) - flux_y[b])
@@ -355,53 +498,25 @@
         for c in range(5):
             finish(c, state[c] - ratio * change[c][:ROWS, :COLS])
 
-        for copy in shared:
-            copy.wait_recv()
-
-        def border(offset):
-            back = AROUND.index((-offset[0], -offset[1]))
-            return line_in[section, back], near[offset] > level
-
-        below, w_below = border((-1, 0))
-        above, w_above = border((1, 0))
-        left, w_left = border((0, -1))
-        right, w_right = border((0, 1))
-        sides = jnp.where(
-            sub8 == 0, left[3:4], jnp.where(sub8 == 1, right[2:3], 0.0)
-        )
-        sides = dot(halves(sides, 0), line_place, ((0,), (0,)))[:24]
+        sides = jnp.where(sub8 == 0, -fine_edge[2:3], jnp.where(sub8 == 1, -fine_edge[6:7], 0.0))
+        sides = jnp.where(in_side, sides, 0.0)
+        sides = dot(halves(sides, 0), line_place, ((0,), (0,)))[80:104]
         row24, lane24 = iota((24, COLS), 0), iota((24, COLS), 1)
         part = edge[:24, :COLS]
         on_low, on_high = row24 == 0, row24 == rows
         on_left, on_right = lane24 == 0, lane24 == cols
 
-        def flag(condition):
-            return jnp.where(condition, 1.0, 0.0).astype(F32)
-
-        part = jnp.where(on_low, flag(w_below) * below[1:2] + (1.0 - flag(w_below)) * part, part)
-        part = jnp.where(on_high, flag(w_above) * above[0:1] + (1.0 - flag(w_above)) * part, part)
-        part = jnp.where(on_left, flag(w_left) * sides + (1.0 - flag(w_left)) * part, part)
-        part = jnp.where(on_right, flag(w_right) * sides + (1.0 - flag(w_right)) * part, part)
-        for vertical, beside, horizontal, v_row, h_row, offset in (
-            ((below, w_below), (left, w_left), (on_low, on_left), 6, 5, (-1, -1)),
-            ((below, w_below), (right, w_right), (on_low, on_right), 7, 4, (-1, 1)),
-            ((above, w_above), (left, w_left), (on_high, on_left), 4, 7, (1, -1)),
-            ((above, w_above), (right, w_right), (on_high, on_right), 5, 6, (1, 1)),
-        ):
-            far, w_far = border(offset)
-            d_row = 11 - (4 + (2 if offset[0] > 0 else 0) + (1 if offset[1] > 0 else 0))
-            a, b, c = flag(vertical[1]), flag(beside[1]), flag(w_far)
-            count = a + b + c
-            share = jnp.where(count > 2.5, jnp.float32(1.0 / 3.0), jnp.where(count > 1.5, 0.5, 1.0))
-            value = share * (
-                a * vertical[0][v_row : v_row + 1]
-                + b * beside[0][h_row : h_row + 1]
-                + c * far[d_row + 0 : d_row + 1]
-            )
-            keep = flag(count < 0.5)
-            part = jnp.where(
-                horizontal[0] & horizontal[1], keep * edge[:24, :COLS] + (1.0 - keep) * value, part
-            )
+        def border_flags(row):
+            side = finer[(row, 0)]
+            first = jnp.maximum(jnp.maximum(side, finer[(0, -1)]), finer[(row, -1)])
+            final = jnp.maximum(jnp.maximum(side, finer[(0, 1)]), finer[(row, 1)])
+            value = jnp.where(on_left, first, jnp.where(on_right, final, side))
+            return jnp.where(lane24 <= cols, value, 0.0) > 0.5
+
+        part = jnp.where(on_left & (finer[(0, -1)] > 0.5), sides, part)
+        part = jnp.where(on_right & (finer[(0, 1)] > 0.5), sides, part)
+        part = jnp.where(on_low & border_flags(-1), fine_edge[2:3], part)
+        part = jnp.where(on_high & border_flags(1), fine_edge[6:7], part)
         top = jnp.concatenate([part, edge[:24, COLS:]], axis=1)
         edge = jnp.concatenate([top, edge[24:]], axis=0)
         finish(5, state[5] - ratio * (roll(edge, -1, 0) - edge)[:ROWS, :COLS])
@@ -426,18 +541,17 @@
             pltpu.SMEM(region_levels.shape, I32),
             pltpu.VMEM((7, 40, 256), F32),
             pltpu.VMEM((7, ROWS, COLS), F32),
-            pltpu.VMEM((2, 2, 32, COLS), F32),
-            pltpu.VMEM((2, 2, 32, COLS), F32),
+            pltpu.VMEM((2, 2, 48, COLS), F32),
+            pltpu.VMEM((2, 2, 48, COLS), F32),
             pltpu.VMEM((2, 6, 8, COLS), F32),
             pltpu.VMEM((2, 6, 8, COLS), F32),
-            pltpu.VMEM((2, 2, 8, COLS), F32),
-            pltpu.VMEM((2, 2, 8, COLS), F32),
-            pltpu.VMEM((2, 8, COLS), F32),
-            pltpu.VMEM((2, 8, 8, COLS), F32),
+            pltpu.VMEM((2, 2, 24, COLS), F32),
+            pltpu.VMEM((2, 2, 24, COLS), F32),
             pltpu.VMEM((6, 256, COLS), BF16),
             pltpu.VMEM((2, 512, 256), BF16),
-            pltpu.SemaphoreType.DMA((2, 16)),
-            pltpu.SemaphoreType.DMA((2, 16)),
+            pltpu.VMEM((512, 256), BF16),
+            pltpu.SemaphoreType.DMA((2, 8)),
+            pltpu.SemaphoreType.DMA((2, 8)),
             pltpu.SemaphoreType.DMA((2,)),
         ],
         compiler_params=pltpu.CompilerParams(

time: 26.9 us -> 18.6 us (0.69)
  Pallas kernels: 26.1 us -> 17.7 us
    pallas_call x1, Pallas kernels: 26.1 us -> 17.7 us  [on_device(): pl.pallas_call(functools.partial(kernel, seg_count, sub_count), out_shape...]
where the time goes in v4:
time: 18.6 us; the launch traced here: 18.4 us
  Pallas kernels  17.7 us (95%)
  local copies, waits for them, and re-layouts  0.65 us (3%)
    pallas_call x1, Pallas kernels, on_device(): pl.pallas_call(functools.partial(kernel, seg_count, sub_count), out_shape...  17.7 us
    unnamed x1, local copies, waits for them, and re-layouts  0.65 us

profile of v4, /device:TPU:0, one launch (start us, length us, event | category | flops | bytes accessed | tf_op | source)
XLA Modules:
  0.0 18.4 jit_solution(17255585761523610618)
XLA Ops:
  0.0 17.7 %shard_map.28 = f32[7,32,128]{2,1,0:T(8,128)S(1)} custom-call(f32[7,32,128]{2,1,0:T(8,128)} %fields_hbm.1, s32[4,8]{1,0:T(4,128)} %bitcast.1), custom_call_target="tpu_custom_call" | custom-call | tf_op jit(solution)/shard_map/pallas_call | solution.py:534
  17.7 0.6 %copy.4 = f32[7,32,128]{2,1,0:T(8,128)} copy(f32[7,32,128]{2,1,0:T(8,128)S(1)} %shard_map.28) | data formatting | bytes 229376

commit v5 on v4

--- a/solution.py
+++ b/solution.py
@@ -121,7 +121,7 @@
 def kernel(
     seg_count, sub_count, fields_hbm, levels_hbm, out,
     fields, levels, ghosted, current, row_out, row_in, corner_out, corner_in, col_out, col_in,
-    lane_maps, row_maps, fine_map, send_sem, recv_sem, fetch_sem,
+    lane_maps, row_maps, fine_map, border_map, send_sem, recv_sem, fetch_sem,
 ):
     fetches = [
         pltpu.make_async_copy(levels_hbm, levels, fetch_sem.at[0]),
@@ -142,6 +142,15 @@
     for target in places:
         pl.semaphore_signal(barrier, inc=1, device_id=target, device_id_type=MESH)
 
+    i, j = iota((COLS, COLS), 0), iota((COLS, COLS), 1)
+    together = (i >> 5) == (j >> 5)
+    comp_six = (i >> 5) == 2
+    source = (i & ~31) + ((i & 31) >> 1) + ((i & 1) << 4)
+    fine_map[...] = twice(jnp.where(source == j, 1.0, 0.0), 0)
+    end = jnp.where(j == 8, 0, jnp.where(j == 9, 1, 2 * COLS))
+    border_map[:, 0:COLS] = twice(jnp.where((i >> 1) + ((i & 1) << 6) == j, 1.0, 0.0), 0)
+    border_map[:, 2 * COLS :] = twice(jnp.where(i == end, 1.0, 0.0), 0)
+
     fetches[0].wait()
     level = levels[sub, seg]
     near = {offset: levels[p[1], p[0]] for offset, p in zip(AROUND, places)}
@@ -150,7 +159,6 @@
     ratio = pick(level, [jnp.float32(STEP_SIZE / h) for h in (4.0, 2.0, 1.0)])
     delta = {offset: near[offset] - level for offset in AROUND}
 
-    i, j = iota((COLS, COLS), 0), iota((COLS, COLS), 1)
     for k, offset in enumerate(AROUND[:6]):
         if offset[1] == 0:
             matrix = resample(i, j, delta[offset])
@@ -161,17 +169,14 @@
             ok = (first >= 0) & (first < 3)
             matrix = jnp.where(ok, resample(i, first, delta[offset]), 0.0)
         lane_maps[k] = twice(matrix, 0)
-    i, j = iota((256, 256), 0), iota((256, 256), 1)
-    together = (i >> 5) == (j >> 5)
-    face_rows = (i >> 5) == 6
+    border_map[:, COLS : 2 * COLS] = twice(jnp.where(i == end + cols - 2, 1.0, 0.0), 0)
     i, j = i & 31, j & 31
     for k, offset in enumerate(AROUND[6:]):
         d = delta[offset]
-        faces = jnp.where(d < 0, jnp.where(i == 2 * j, 1.0, 0.0), resample(i, j, d))
-        matrix = jnp.where(together, jnp.where(face_rows, faces, resample(i, j, d)), 0.0)
-        row_maps[k] = twice(matrix, 0)
-    source = (i >> 1) + ((i & 1) << 4)
-    fine_map[...] = twice(jnp.where(together, jnp.where(source == j, 1.0, 0.0), 0.0), 0)
+        matrix = jnp.where(together, resample(i, j, d), 0.0)
+        row_maps[k, 0] = twice(matrix, 0)
+        faces = jnp.where(together, jnp.where(i == 2 * j, 1.0, 0.0), 0.0)
+        row_maps[k, 1] = twice(jnp.where(comp_six & (d < 0), faces, matrix), 0)
     k, i = iota((16, COLS), 0), iota((16, COLS), 1)
     to_right = k >= 8
     k = k & 7
@@ -199,19 +204,6 @@
         + jnp.where((k >= 8) & (k < 11) & (i == cols + k - 8), 1.0, 0.0),
         0,
     )
-    i, j = iota((COLS, COLS), 0), iota((COLS, COLS), 1)
-    end = jnp.where(j == 8, 0, jnp.where(j == 9, 1, 2 * COLS))
-    border_map = twice(
-        jnp.concatenate(
-            [
-                jnp.where((i >> 1) + ((i & 1) << 6) == j, 1.0, 0.0),
-                jnp.where(i == end + cols - 2, 1.0, 0.0),
-                jnp.where(i == end, 1.0, 0.0),
-            ],
-            axis=1,
-        ),
-        0,
-    )
     k, i = iota((8, COLS), 0), iota((8, COLS), 1)
     line_place = twice(
         jnp.where(((k == 0) & (i == 0)) | ((k == 1) & (i == cols)), 1.0, 0.0), 0
@@ -265,62 +257,49 @@
             state = [current[c] for c in range(7)]
 
         halo = []
-        for k, offset in enumerate(AROUND[6:]):
-            if k == 0:
-                stacked = jnp.concatenate(state + [jnp.zeros((ROWS, COLS), F32)], axis=0)
-                columns = dot(column_map, halves(stacked, 1), ((1,), (1,)))
-                lane = iota((8, 256), 1) >> 5
-            part = columns[8 * k : 8 * k + 8]
-            fine = dot(halves(part, 1), fine_map[...])
-            col_out[section, k, 8:16] = jnp.where(
-                upper8, fine[:, :COLS], roll(fine[:, COLS:], 4, 0)
+        tops = [pick(level, (v[0:8], v[8:16], v[24:32])) for v in state]
+        lows = [v[0:8] for v in state]
+        border = [
+            jnp.where(
+                sub8 < 2,
+                roll(top, 2, 0),
+                jnp.where(
+                    sub8 < 4,
+                    roll(low, 2, 0),
+                    jnp.where(sub8 < 6, roll(top, 6, 0), roll(low, 6, 0)),
+                ),
             )
-            part = jnp.where(lane == 5, roll(part, -3, 0), part)
-            part = dot(halves(part, 1), row_maps[k])
-            col_out[section, k, 0:8] = jnp.where(
-                upper8, roll(part[:, COLS:], 4, 0), part[:, :COLS]
-            )
-        border = []
-        for v in state:
-            top = pick(level, (v[0:8], v[8:16], v[24:32]))
-            border.append(
-                jnp.where(
-                    sub8 < 2,
-                    roll(top, 2, 0),
-                    jnp.where(
-                        sub8 < 4,
-                        roll(v[0:8], 2, 0),
-                        jnp.where(sub8 < 6, roll(top, 6, 0), roll(v[0:8], 6, 0)),
-                    ),
-                )
-            )
-        border = dot(halves(jnp.concatenate(border, axis=0), 1), border_map)
+            for top, low in zip(tops, lows)
+        ]
+        stacked = jnp.concatenate(state + [jnp.zeros((ROWS, COLS), F32)], axis=0)
+        columns = dot(column_map, halves(stacked, 1), ((1,), (1,)))
+        border = dot(halves(jnp.concatenate(border, axis=0), 1), border_map[...])
         ends = []
         for part in (border[:, COLS : 2 * COLS], border[:, 2 * COLS :]):
             total = part[0:8]
             for c in range(1, 7):
                 total = total + roll(part[8 * c : 8 * c + 8], 16 * c, 1)
             ends.append(total)
-        col_out[section, 0, 16:24] = ends[1]
-        col_out[section, 1, 16:24] = ends[0]
-        for group in range(2):
-            up = down = jnp.zeros((8, COLS), F32)
-            for q in range(4 if group == 0 else 3):
-                c = 4 * group + q
-                part = roll(border[8 * c : 8 * c + 8, :COLS], 2 * q, 0)
-                up = jnp.where((sub8 >> 1) == q, part, up)
-                down = jnp.where((sub8 >> 1) == ((3 + q) & 3), part, down)
-            row_out[section, 0, 32 + 8 * group : 40 + 8 * group] = up
-            row_out[section, 1, 32 + 8 * group : 40 + 8 * group] = down
+        for k in range(2):
+            part = columns[8 * k : 8 * k + 8]
+            first, second = part[:, :COLS], part[:, COLS:]
+            fine = dot(
+                jnp.concatenate([halves(first, 1), halves(second, 1)], axis=0), fine_map[...]
+            )
+            col_out[section, k, 8:16] = jnp.where(upper8, fine[:8], roll(fine[8:], 4, 0))
+            second = jnp.where((lane8 >> 5) == 1, roll(second, -3, 0), second)
+            first = dot(halves(first, 1), row_maps[k, 0])
+            second = dot(halves(second, 1), row_maps[k, 1])
+            col_out[section, k, 0:8] = jnp.where(upper8, roll(second, 4, 0), first)
+            col_out[section, k, 16:24] = ends[1 - k]
+        if section == 0:
+            pl.semaphore_wait(barrier, len(AROUND))
+        for k in range(2):
+            halo.append(send(section, 6 + k, col_out.at[section, k], col_in.at[section, k]))
         for upper in (True, False):
-            if upper:
-                block = [
-                    pick(level, (v[0:8], v[8:16], v[24:32])) for v in state
-                ]
-            else:
-                block = [v[0:8] for v in state]
-            choices = strip_choices(block, upper, sub8, odd_lane)
-            for k in range(0, 3) if upper else range(3, 6):
+            choices = strip_choices(tops if upper else lows, upper, sub8, odd_lane)
+            base = 0 if upper else 3
+            for k in (base + 1, base + 2, base):
                 d = delta[AROUND[k]]
                 chosen = [
                     jnp.where(d == 0, a, jnp.where(d < 0, b, c)) for a, b, c in zip(*choices)
@@ -332,23 +311,27 @@
                 ]
                 packed = jnp.concatenate(packed, axis=0)
                 packed = dot(halves(packed, 1), lane_maps[k])
-                if k % 3 == 0:
-                    row_out[section, k // 3, 0:32] = packed
-                else:
-                    corner = packed[0:8]
+                if k != base:
+                    corner = packed[0:8] + ends[k - base - 1]
                     for m in range(1, 4):
                         corner = corner + roll(packed[8 * m : 8 * m + 8], 32 * m, 1)
-                    corner_out[section, k] = corner + ends[0 if k % 3 == 1 else 1]
-        if section == 0:
-            pl.semaphore_wait(barrier, len(AROUND))
-        for k in range(2):
-            halo.append(send(section, 6 + k, col_out.at[section, k], col_in.at[section, k]))
-        for k in (1, 2, 4, 5):
-            halo.append(send(section, k, corner_out.at[section, k], corner_in.at[section, k]))
-        for k in (0, 3):
-            halo.append(
-                send(section, k, row_out.at[section, k // 3], row_in.at[section, k // 3])
-            )
+                    corner_out[section, k] = corner
+                    halo.append(
+                        send(section, k, corner_out.at[section, k], corner_in.at[section, k])
+                    )
+                    continue
+                row_out[section, k // 3, 0:32] = packed
+                for group in range(2):
+                    block = jnp.zeros((8, COLS), F32)
+                    for q in range(4 if group == 0 else 3):
+                        c = 4 * group + q
+                        part = roll(border[8 * c : 8 * c + 8, :COLS], 2 * q, 0)
+                        place_of = q if upper else (3 + q) & 3
+                        block = jnp.where((sub8 >> 1) == place_of, part, block)
+                    row_out[section, k // 3, 32 + 8 * group : 40 + 8 * group] = block
+                halo.append(
+                    send(section, k, row_out.at[section, k // 3], row_in.at[section, k // 3])
+                )
         for copy in halo:
             copy.wait_recv()
 
@@ -393,10 +376,18 @@
         field_z, face_x, face_y = ghosted[4], ghosted[5], ghosted[6]
         centre_x = 0.5 * (face_x + roll(face_x, -1, 1))
         centre_y = 0.5 * (face_y + roll(face_y, -1, 0))
-        flux_x = sweep([density, speed_x, speed_y, speed_z, centre_y, field_z], face_x, 1)
-        flux_y = sweep([density, speed_y, speed_x, speed_z, centre_x, field_z], face_y, 0)
+        prims_x = [density, speed_x, speed_y, speed_z, centre_y, field_z]
+        prims_y = [density, speed_y, speed_x, speed_z, centre_x, field_z]
+        flux_x = sweep([v[:ROWS] for v in prims_x], face_x[:ROWS], 1)
+        prims_x[3] = None
+        ghost_x = sweep([v if v is None else v[ROWS:] for v in prims_x], face_x[ROWS:], 1)
+        flux_y = sweep([v[:, :COLS] for v in prims_y], face_y[:, :COLS], 0)
+        prims_y[3] = None
+        ghost_y = sweep([v if v is None else v[:, COLS:] for v in prims_y], face_y[:, COLS:], 0)
+        cross_x = jnp.concatenate([flux_x[4], ghost_x[4]], axis=0)
+        cross_y = jnp.concatenate([flux_y[4], ghost_y[4]], axis=1)
         edge = 0.25 * (
-            (flux_y[4] + roll(flux_y[4], 1, 1)) - (flux_x[4] + roll(flux_x[4], 1, 0))
+            (cross_y + roll(cross_y, 1, 1)) - (cross_x + roll(cross_x, 1, 0))
         )
         edge = jnp.where(corner_ok, edge, 0.0)
 
@@ -485,7 +476,8 @@
         fine_edge = 0.25 * (fine_y - (fine_x + roll(fine_x, 1, 0)))
 
         change = [
-            (roll(flux_x[a], -1, 1) - flux_x[a]) + (roll(flux_y[b], -1, 0) - flux_y[b])
+            (roll(flux_x[a], -1, 1) - flux_x[a])[:, :COLS]
+            + (roll(flux_y[b], -1, 0) - flux_y[b])[:ROWS]
             for a, b in ((0, 0), (1, 2), (2, 1), (3, 3), (5, 5))
         ]
 
@@ -496,7 +488,7 @@
                 out[c] = jnp.where(cell_ok, 0.5 * (fields[c] + value), 0.0)
 
         for c in range(5):
-            finish(c, state[c] - ratio * change[c][:ROWS, :COLS])
+            finish(c, state[c] - ratio * change[c])
 
         sides = jnp.where(sub8 == 0, -fine_edge[2:3], jnp.where(sub8 == 1, -fine_edge[6:7], 0.0))
         sides = jnp.where(in_side, sides, 0.0)
@@ -548,8 +540,9 @@
             pltpu.VMEM((2, 2, 24, COLS), F32),
             pltpu.VMEM((2, 2, 24, COLS), F32),
             pltpu.VMEM((6, 256, COLS), BF16),
-            pltpu.VMEM((2, 512, 256), BF16),
-            pltpu.VMEM((512, 256), BF16),
+            pltpu.VMEM((2, 2, 256, COLS), BF16),
+            pltpu.VMEM((256, COLS), BF16),
+            pltpu.VMEM((256, 3 * COLS), BF16),
             pltpu.SemaphoreType.DMA((2, 8)),
             pltpu.SemaphoreType.DMA((2, 8)),
             pltpu.SemaphoreType.DMA((2,)),

time: 18.6 us -> 18.8 us (1.011)
  Pallas kernels: 17.7 us -> 18 us
    pallas_call x1, Pallas kernels: 17.7 us -> 18 us  [on_device(): pl.pallas_call(functools.partial(kernel, seg_count, sub_count), out_shape...]
where the time goes in v5:
time: 18.8 us; the launch traced here: 18.6 us
  Pallas kernels  18 us (96%)
  local copies, waits for them, and re-layouts  0.65 us (3%)
    pallas_call x1, Pallas kernels, on_device(): pl.pallas_call(functools.partial(kernel, seg_count, sub_count), out_shape...  18 us
    unnamed x1, local copies, waits for them, and re-layouts  0.65 us

profile of v5, /device:TPU:0, one launch (start us, length us, event | category | flops | bytes accessed | tf_op | source)
XLA Modules:
  0.0 18.6 jit_solution(1819746376123839328)
XLA Ops:
  0.0 18.0 %shard_map.28 = f32[7,32,128]{2,1,0:T(8,128)S(1)} custom-call(f32[7,32,128]{2,1,0:T(8,128)} %fields_hbm.1, s32[4,8]{1,0:T(4,128)} %bitcast.1), custom_call_target="tpu_custom_call" | custom-call | tf_op jit(solution)/shard_map/pallas_call | solution.py:526
  18.0 0.6 %copy.4 = f32[7,32,128]{2,1,0:T(8,128)} copy(f32[7,32,128]{2,1,0:T(8,128)S(1)} %shard_map.28) | data formatting | bytes 229376

commit v6 on v5

--- a/solution.py
+++ b/solution.py
@@ -247,7 +247,6 @@
             device_id_type=MESH,
         )
         copy.start()
-        copies.append(copy)
         return copy
 
     for section in range(2):
@@ -256,7 +255,6 @@
         else:
             state = [current[c] for c in range(7)]
 
-        halo = []
         tops = [pick(level, (v[0:8], v[8:16], v[24:32])) for v in state]
         lows = [v[0:8] for v in state]
         border = [
@@ -286,16 +284,11 @@
             fine = dot(
                 jnp.concatenate([halves(first, 1), halves(second, 1)], axis=0), fine_map[...]
             )
-            col_out[section, k, 8:16] = jnp.where(upper8, fine[:8], roll(fine[8:], 4, 0))
+            col_out[section, k, 8:16] = by_sublane(roll(fine[8:], 2, 0), ends[1 - k], fine[:8])
             second = jnp.where((lane8 >> 5) == 1, roll(second, -3, 0), second)
             first = dot(halves(first, 1), row_maps[k, 0])
             second = dot(halves(second, 1), row_maps[k, 1])
             col_out[section, k, 0:8] = jnp.where(upper8, roll(second, 4, 0), first)
-            col_out[section, k, 16:24] = ends[1 - k]
-        if section == 0:
-            pl.semaphore_wait(barrier, len(AROUND))
-        for k in range(2):
-            halo.append(send(section, 6 + k, col_out.at[section, k], col_in.at[section, k]))
         for upper in (True, False):
             choices = strip_choices(tops if upper else lows, upper, sub8, odd_lane)
             base = 0 if upper else 3
@@ -316,9 +309,6 @@
                     for m in range(1, 4):
                         corner = corner + roll(packed[8 * m : 8 * m + 8], 32 * m, 1)
                     corner_out[section, k] = corner
-                    halo.append(
-                        send(section, k, corner_out.at[section, k], corner_in.at[section, k])
-                    )
                     continue
                 row_out[section, k // 3, 0:32] = packed
                 for group in range(2):
@@ -329,10 +319,22 @@
                         place_of = q if upper else (3 + q) & 3
                         block = jnp.where((sub8 >> 1) == place_of, part, block)
                     row_out[section, k // 3, 32 + 8 * group : 40 + 8 * group] = block
-                halo.append(
-                    send(section, k, row_out.at[section, k // 3], row_in.at[section, k // 3])
-                )
-        for copy in halo:
+        if section == 0:
+            pl.semaphore_wait(barrier, len(AROUND))
+        done, copies = copies, []
+        for k in range(2):
+            copies.append(send(section, 6 + k, col_out.at[section, k], col_in.at[section, k]))
+        for k in (1, 2, 4, 5):
+            copies.append(
+                send(section, k, corner_out.at[section, k], corner_in.at[section, k])
+            )
+        for k in (0, 3):
+            copies.append(
+                send(section, k, row_out.at[section, k // 3], row_in.at[section, k // 3])
+            )
+        for copy in done:
+            copy.wait_send()
+        for copy in copies:
             copy.wait_recv()
 
         received = jnp.concatenate(
@@ -392,16 +394,16 @@
         edge = jnp.where(corner_ok, edge, 0.0)
 
         from_left = by_sublane(
-            corner_in[section, 1], col_in[section, 1, 16:24], corner_in[section, 4]
+            corner_in[section, 1], col_in[section, 1, 8:16], corner_in[section, 4]
         )
         from_right = by_sublane(
-            corner_in[section, 2], col_in[section, 0, 16:24], corner_in[section, 5]
+            corner_in[section, 2], col_in[section, 0, 8:16], corner_in[section, 5]
         )
         from_right = jnp.where(level == 0, roll(from_right, 32, 1), roll(from_right, 64, 1))
         beside = []
         for k in (1, 0):
             part = col_in[section, k, 8:16]
-            part = jnp.concatenate([part, roll(part, 4, 0)], axis=1)
+            part = jnp.concatenate([part, roll(part, -2, 0)], axis=1)
             beside.append(roll(part, 2, 0) if k == 1 else part)
         own_sides = jnp.where(sub8[:, :1] < 4, columns[6:7], columns[15:16])
         sub_wide = iota((8, 256), 0)
@@ -537,8 +539,8 @@
             pltpu.VMEM((2, 2, 48, COLS), F32),
             pltpu.VMEM((2, 6, 8, COLS), F32),
             pltpu.VMEM((2, 6, 8, COLS), F32),
-            pltpu.VMEM((2, 2, 24, COLS), F32),
-            pltpu.VMEM((2, 2, 24, COLS), F32),
+            pltpu.VMEM((2, 2, 16, COLS), F32),
+            pltpu.VMEM((2, 2, 16, COLS), F32),
             pltpu.VMEM((6, 256, COLS), BF16),
             pltpu.VMEM((2, 2, 256, COLS), BF16),
             pltpu.VMEM((256, COLS), BF16),

time: 18.8 us -> 18.1 us (0.963)
  Pallas kernels: 18 us -> 17.3 us
    pallas_call x1, Pallas kernels: 18 us -> 17.3 us  [on_device(): pl.pallas_call(functools.partial(kernel, seg_count, sub_count), out_shape...]
where the time goes in v6:
time: 18.1 us; the launch traced here: 18 us
  Pallas kernels  17.3 us (96%)
  local copies, waits for them, and re-layouts  0.65 us (4%)
    pallas_call x1, Pallas kernels, on_device(): pl.pallas_call(functools.partial(kernel, seg_count, sub_count), out_shape...  17.3 us
    unnamed x1, local copies, waits for them, and re-layouts  0.65 us

profile of v6, /device:TPU:0, one launch (start us, length us, event | category | flops | bytes accessed | tf_op | source)
XLA Modules:
  0.0 18.0 jit_solution(1860945988801218220)
XLA Ops:
  0.0 17.3 %shard_map.28 = f32[7,32,128]{2,1,0:T(8,128)S(1)} custom-call(f32[7,32,128]{2,1,0:T(8,128)} %fields_hbm.1, s32[4,8]{1,0:T(4,128)} %bitcast.1), custom_call_target="tpu_custom_call" | custom-call | tf_op jit(solution)/shard_map/pallas_call | solution.py:528
  17.3 0.6 %copy.4 = f32[7,32,128]{2,1,0:T(8,128)} copy(f32[7,32,128]{2,1,0:T(8,128)S(1)} %shard_map.28) | data formatting | bytes 229376

commit v7 on v6

--- a/solution.py
+++ b/solution.py
@@ -52,6 +52,22 @@
 
 
 def sweep(primitives, normal, axis):
+    chunks = [slice(row, row + 8) for row in range(0, normal.shape[0], 8)]
+
+    def part(values, rows):
+        return [None if v is None else v[rows] for v in values]
+
+    if axis == 1:
+        pieces = [
+            riemann(*reconstruct(part(primitives, rows), axis), normal[rows]) for rows in chunks
+        ]
+    else:
+        left, right = reconstruct(primitives, axis)
+        pieces = [riemann(part(left, rows), part(right, rows), normal[rows]) for rows in chunks]
+    return [None if v[0] is None else jnp.concatenate(v, axis=0) for v in zip(*pieces)]
+
+
+def reconstruct(primitives, axis):
     left, right = [], []
     for value in primitives:
         if value is None:
@@ -63,7 +79,7 @@
         left.append(roll(value + half, 1, axis))
         right.append(value - half)
 
-    return riemann(left, right, normal)
+    return left, right
 
 
 def riemann(left, right, normal):

time: 18.1 us -> 18.1 us (level)
  no operation moved by 1% of the time
where the time goes in v7:
time: 18.1 us; the launch traced here: 18 us
  Pallas kernels  17.3 us (96%)
  local copies, waits for them, and re-layouts  0.65 us (4%)
    pallas_call x1, Pallas kernels, on_device(): pl.pallas_call(functools.partial(kernel, seg_count, sub_count), out_shape...  17.3 us
    unnamed x1, local copies, waits for them, and re-layouts  0.65 us

profile of v7, /device:TPU:0, one launch (start us, length us, event | category | flops | bytes accessed | tf_op | source)
XLA Modules:
  0.0 18.0 jit_solution(14957507653736341025)
XLA Ops:
  0.0 17.3 %shard_map.28 = f32[7,32,128]{2,1,0:T(8,128)S(1)} custom-call(f32[7,32,128]{2,1,0:T(8,128)} %fields_hbm.1, s32[4,8]{1,0:T(4,128)} %bitcast.1), custom_call_target="tpu_custom_call" | custom-call | tf_op jit(solution)/shard_map/pallas_call | solution.py:544
  17.3 0.6 %copy.4 = f32[7,32,128]{2,1,0:T(8,128)} copy(f32[7,32,128]{2,1,0:T(8,128)S(1)} %shard_map.28) | data formatting | bytes 229376

commit v8 on v6

--- a/solution.py
+++ b/solution.py
@@ -127,8 +127,6 @@
         pltpu.make_async_copy(levels_hbm, levels, fetch_sem.at[0]),
         pltpu.make_async_copy(fields_hbm, fields, fetch_sem.at[1]),
     ]
-    for fetch in fetches:
-        fetch.start()
     seg, sub = lax.axis_index("seg"), lax.axis_index("sub")
 
     def place(offset):
@@ -141,6 +139,8 @@
     barrier = pltpu.get_barrier_semaphore()
     for target in places:
         pl.semaphore_signal(barrier, inc=1, device_id=target, device_id_type=MESH)
+    for fetch in fetches:
+        fetch.start()
 
     i, j = iota((COLS, COLS), 0), iota((COLS, COLS), 1)
     together = (i >> 5) == (j >> 5)
@@ -289,6 +289,10 @@
             first = dot(halves(first, 1), row_maps[k, 0])
             second = dot(halves(second, 1), row_maps[k, 1])
             col_out[section, k, 0:8] = jnp.where(upper8, roll(second, 4, 0), first)
+        done, copies = copies, []
+        if section == 1:
+            for k in range(2):
+                copies.append(send(section, 6 + k, col_out.at[section, k], col_in.at[section, k]))
         for upper in (True, False):
             choices = strip_choices(tops if upper else lows, upper, sub8, odd_lane)
             base = 0 if upper else 3
@@ -321,9 +325,8 @@
                     row_out[section, k // 3, 32 + 8 * group : 40 + 8 * group] = block
         if section == 0:
             pl.semaphore_wait(barrier, len(AROUND))
-        done, copies = copies, []
-        for k in range(2):
-            copies.append(send(section, 6 + k, col_out.at[section, k], col_in.at[section, k]))
+            for k in range(2):
+                copies.append(send(section, 6 + k, col_out.at[section, k], col_in.at[section, k]))
         for k in (1, 2, 4, 5):
             copies.append(
                 send(section, k, corner_out.at[section, k], corner_in.at[section, k])

time: 18.1 us -> 18.1 us (level)
  no operation moved by 1% of the time
where the time goes in v8:
time: 18.1 us; the launch traced here: 17.9 us
  Pallas kernels  17.3 us (96%)
  local copies, waits for them, and re-layouts  0.65 us (4%)
    pallas_call x1, Pallas kernels, on_device(): pl.pallas_call(functools.partial(kernel, seg_count, sub_count), out_shape...  17.3 us
    unnamed x1, local copies, waits for them, and re-layouts  0.65 us

profile of v8, /device:TPU:0, one launch (start us, length us, event | category | flops | bytes accessed | tf_op | source)
XLA Modules:
  0.0 17.9 jit_solution(14718692470773703145)
XLA Ops:
  0.0 17.3 %shard_map.28 = f32[7,32,128]{2,1,0:T(8,128)S(1)} custom-call(f32[7,32,128]{2,1,0:T(8,128)} %fields_hbm.1, s32[4,8]{1,0:T(4,128)} %bitcast.1), custom_call_target="tpu_custom_call" | custom-call | tf_op jit(solution)/shard_map/pallas_call | solution.py:531
  17.3 0.6 %copy.4 = f32[7,32,128]{2,1,0:T(8,128)} copy(f32[7,32,128]{2,1,0:T(8,128)S(1)} %shard_map.28) | data formatting | bytes 229376
